TPU v7x, 32 devices: a whole 2x2x4 slice. The times are simulated.
32 devices in a mesh: grp: 4 (over z), dev: 8 (over y, x, core).
Axes of the slice: x: 2, y: 2, z: 4, core: 2. Of those that a mesh axis runs over, the one named last changes fastest.
Arguments:
- adjoint: bfloat16 [16384, 384], P(('grp', 'dev')), may hold values from -6 to 6
- state: bfloat16 [16384, 384], P(('grp', 'dev')), may hold values from -6 to 6
- interp: bfloat16 [64, 64], replicated, may hold values from -0.75 to 0.75
- flux_weights: float32 [3, 6, 6], replicated, may hold values from -2.5 to 2.5
- metric: float32 [16384, 64], P(('grp', 'dev')), may hold values from 0.3 to 3
- geometry: float32 [3, 64, 64], replicated, may hold values from -0.375 to 0.375
- connectivity: int32 [16384, 64], P(('grp', 'dev')), may hold values from 0 to 8415
- halo_source: int32 [256, 64], P(('grp', 'dev')), may hold values from 0 to 224, as said below
- halo_target: int32 [256, 64], P(('grp', 'dev')), may hold values from 0 to 8191
- surface_node: int32 [4096], P(('grp', 'dev')), may hold values from 0 to 8191
- surface_point: int32 [4096], P(('grp', 'dev')), may hold values from 0 to 39999
- point_coords: float32 [3, 40000], replicated, may hold values from 0 to 1
Outputs:
- node_partials: float32 [3, 262144], P(None, ('grp', 'dev'))
- point_gradient: float32 [3, 40000], P(None, 'grp')
Inputs may be any that keep to these rules, and one draw needn't show every extreme that they name: `halo_source`: on each device, the row of the device itself holds only 224; every halo copy 0 to 223 stands in exactly one slot of the other rows; all other slots hold 224.
All inputs are finite; a program needn't handle non-finite values.
Results may differ from a plain program's by a relative error of at most 0.0003.
Values sent between devices are 32-bit elements; how exact they have to be, the bound alone decides.
No kernel may reach another device: no remote copies, remote signals or barrier semaphores. Data moves between devices by JAX's collectives and lax.ppermute only.
A program may use at most 768 MiB of HBM per device.

v0:
```python
import jax
import jax.numpy as jnp
from jax import lax
from jax.sharding import PartitionSpec as P

NCP = 40000
ITERS = 2
NOWN = 8192


ridge_weight = 4.0


def support_radius():
    return (168.0 / (4.18879 * NCP)) ** (1.0 / 3.0)


def wendland(row_coords, col_coords):
    dist_squared = jnp.zeros((row_coords.shape[1], col_coords.shape[1]), jnp.float32)
    for axis_number in range(3):
        differ = row_coords[axis_number][:, None] - col_coords[axis_number][None, :]
        dist_squared = dist_squared + differ * differ
    scaled = jnp.sqrt(dist_squared) / support_radius()
    remaining = jnp.maximum(1.0 - scaled, 0.0)
    return remaining**4 * (4.0 * scaled + 1.0)


def element_partials(
    adjoint_rows,
    state_rows,
    metric_rows,
    connectivity_rows,
    interp,
    flux_weights,
    geometry,
    segment_total,
):
    elements = adjoint_rows.shape[0]
    basis_count = interp.shape[0]
    quad_points = interp.shape[1]
    variables = adjoint_rows.shape[1] // basis_count
    elem_nodes = geometry.shape[2]
    adjoint_quad = jnp.dot(
        adjoint_rows.reshape(elements * variables, basis_count),
        interp,
        preferred_element_type=jnp.float32,
    ).reshape(elements, variables, quad_points)
    state_quad = jnp.dot(
        state_rows.reshape(elements * variables, basis_count),
        interp,
        preferred_element_type=jnp.float32,
    ).reshape(elements, variables, quad_points)
    coupled = jnp.einsum("cvw,ewq->ecvq", flux_weights, state_quad, precision=lax.Precision.HIGHEST)
    weighted = jnp.sum(adjoint_quad[:, None] * coupled, axis=2) * metric_rows[:, None, :]
    partials = jnp.einsum("ecq,cqn->ecn", weighted, geometry, precision=lax.Precision.HIGHEST)
    nodal_sums = jax.ops.segment_sum(
        partials.transpose(0, 2, 1).reshape(elements * elem_nodes, 3),
        connectivity_rows.reshape(-1),
        num_segments=segment_total,
    )
    return nodal_sums.T


def squares(residual):
    return lax.psum(jnp.sum(residual * residual, axis=1), "grp")


def on_device(
    adjoint,
    state,
    interp,
    flux_weights,
    metric,
    geometry,
    connectivity,
    halo_source,
    halo_target,
    surface_node,
    surface_point,
    point_coords,
):
    member_count = lax.axis_size("dev")
    group_count = lax.axis_size("grp")
    group_index = lax.axis_index("grp")
    member_index = lax.axis_index("dev")
    halo_count = halo_source.shape[1] * (member_count - 1) // 2
    nodal_sums = element_partials(
        adjoint, state, metric, connectivity, interp, flux_weights, geometry, NOWN + halo_count
    )
    halo_values = jnp.concatenate([nodal_sums[:, NOWN:], jnp.zeros((3, 1), jnp.float32)], axis=1)
    outgoing = halo_values[:, halo_source]
    incoming = lax.all_to_all(outgoing, "dev", split_axis=1, concat_axis=1, tiled=True)
    added = jax.ops.segment_sum(
        incoming.reshape(3, -1).T, halo_target.reshape(-1), num_segments=NOWN
    )
    owned = nodal_sums[:, :NOWN] + added.T
    surface_values = owned[:, surface_node].T
    block_rows = NCP // group_count
    tile_cols = NCP // member_count
    values = lax.all_gather(surface_values, ("grp", "dev"), axis=0, tiled=True)
    points = lax.all_gather(surface_point, ("grp", "dev"), axis=0, tiled=True)
    local = points - group_index * block_rows
    inside = (local >= 0) & (local < block_rows)
    slot_index = jnp.where(inside, local, block_rows)
    right_side = jax.ops.segment_sum(values, slot_index, num_segments=block_rows + 1)[:block_rows].T
    row_coords = lax.dynamic_slice_in_dim(point_coords, group_index * block_rows, block_rows, 1)
    col_coords = lax.dynamic_slice_in_dim(point_coords, member_index * tile_cols, tile_cols, 1)
    sub_count = [divisor for divisor in (8, 5, 4, 2, 1) if block_rows % divisor == 0][0]
    row_parts = row_coords.reshape(3, sub_count, block_rows // sub_count).transpose(1, 0, 2)
    contract = (((1,), (1,)), ((), ()))

    def kernel_part(part_coords):
        return wendland(part_coords, col_coords)

    kernel_tile = lax.map(kernel_part, row_parts).reshape(block_rows, tile_cols)
    solution = jnp.zeros((3, block_rows), jnp.float32)
    residual = right_side
    direction = right_side
    norm_now = squares(residual)
    for iteration in range(ITERS):
        whole = lax.all_gather(direction, "grp", axis=1, tiled=True)
        fetched = lax.dynamic_slice_in_dim(whole, member_index * tile_cols, tile_cols, 1)
        partial_value = lax.dot_general(
            fetched, kernel_tile, contract, precision=lax.Precision.HIGHEST
        )
        image = lax.psum(partial_value, "dev") + ridge_weight * direction
        curvature = lax.psum(jnp.sum(direction * image, axis=1), "grp")
        step_size = norm_now / curvature
        solution = solution + step_size[:, None] * direction
        residual = residual - step_size[:, None] * image
        norm_next = squares(residual)
        direction = residual + (norm_next / norm_now)[:, None] * direction
        norm_now = norm_next
    return (owned, solution)


def solution(mesh):
    in_specs = (
        P(("grp", "dev"), None),
        P(("grp", "dev"), None),
        P(),
        P(),
        P(("grp", "dev"), None),
        P(),
        P(("grp", "dev"), None),
        P(("grp", "dev"), None),
        P(("grp", "dev"), None),
        P(("grp", "dev")),
        P(("grp", "dev")),
        P(),
    )
    out_specs = (P(None, ("grp", "dev")), P(None, "grp"))
    return jax.shard_map(
        on_device, mesh=mesh, in_specs=in_specs, out_specs=out_specs, check_vma=False
    )
```

profile of v0, /device:TPU:0, one launch (start us, length us, event | category | flops | bytes accessed | tf_op | source)
XLA Modules:
  0.0 1226.2 jit_solution(14818749862417003498)
XLA Ops:
  7.2 1.2 copy.66
  8.4 1.0 fusion.22
  10.0 1.2 copy.69
  11.1 1.0 convolution_bitcast_fusion
  12.2 4.6 fusion.3
  16.8 1.1 broadcast_multiply_fusion
  17.8 1.5 convolution_bitcast_fusion.1
  19.4 13.7 %copy.93 = f32[512,64,3]{2,1,0:T(8,128)} copy(f32[512,64,3]{0,1,2:T(8,128)S(1)} %convolution_bitcast_fusion.1) | data formatting | bytes 786432 | tf_op jit(solution)/shard_map/reshape | solution.py:57
  33.3 176.5 %scatter_custom_fusion = f32[8416,3]{1,0:T(8,128)} fusion(s32[32768]{0:T(1024)S(1)} %reshape.290, f32[32768,3]{1,0:T(8,128)} %bitcast.99, f32[]{:T(128)} %constant.63.clone.1), kind=kCustom, calls=%fused_computation.17 | custom fusion | flops 98304 | bytes 101504 | tf_op jit(solution)/shard_map/scatter-add | solution.py:56
  209.9 0.9 slice.56
  210.9 1.0 gather_fusion
  212.1 0.7 reshape.340
  212.8 5.2 all-to-all-start
  218.9 177.6 %while.12 = (s32[]{:T(128)}, f32[8,1250,5000]{2,1,0:T(8,128)}, f32[8,3,1250]{2,0,1:T(8,128)S(1)}, f32[3,5000]{1,0:T(4,128)S(1)}, s32[]{:T(128)}, /*index=5*/s32[]{:T(128)}, s32[]{}, s32[]{}) while((s32[]{:T(128)}, f32[8,1250,5000]{2,1,0:T(8,128)}, f32[8,3,1250]{2,0,1:T(8,128)S(1)}, f32[3,5000]{1,0:T(4,128)S(1)}, s32[]{:T(128)}, ...), condition=%wide.region_7.8_spmd, body=%wide.region_6.7_spmd.sunk | while | flops 100000000 | bytes 25948512 | solution.py:115
  219.1 22.1 %multiply_dynamic-update-slice_fusion.2 = f32[8,1250,5000]{2,1,0:T(8,128)} fusion(f32[8,1250,5000]{2,1,0:T(8,128)} %get-tuple-element.146, s32[]{:T(128)} %get-tuple-element.145, f32[5000]{0:T(1024)S(1)} %bitcast.103, f32[1250]{0:T(1024)S(1)} %get-tuple-element.132, f32[5000]{0:T(1024)S(1)} %bitcast.104, f32[1250]{0:T(1024)S(1)} %get-tuple-element.134, ...), kind=kLoop, calls=%fused_computation.5.clone.1 | loop fusion | flops 100000000 | bytes 25798392 | tf_op jit(solution)/shard_map/while/body/jit(dynamic_update_index_in_dim)/dynamic_update_slice | solution.py:115
  241.3 22.1 %multiply_dynamic-update-slice_fusion.2 = f32[8,1250,5000]{2,1,0:T(8,128)} fusion(f32[8,1250,5000]{2,1,0:T(8,128)} %get-tuple-element.146, s32[]{:T(128)} %get-tuple-element.145, f32[5000]{0:T(1024)S(1)} %bitcast.103, f32[1250]{0:T(1024)S(1)} %get-tuple-element.132, f32[5000]{0:T(1024)S(1)} %bitcast.104, f32[1250]{0:T(1024)S(1)} %get-tuple-element.134, ...), kind=kLoop, calls=%fused_computation.5.clone.1 | loop fusion | flops 100000000 | bytes 25798392 | tf_op jit(solution)/shard_map/while/body/jit(dynamic_update_index_in_dim)/dynamic_update_slice | solution.py:115
  263.5 22.1 %multiply_dynamic-update-slice_fusion.2 = f32[8,1250,5000]{2,1,0:T(8,128)} fusion(f32[8,1250,5000]{2,1,0:T(8,128)} %get-tuple-element.146, s32[]{:T(128)} %get-tuple-element.145, f32[5000]{0:T(1024)S(1)} %bitcast.103, f32[1250]{0:T(1024)S(1)} %get-tuple-element.132, f32[5000]{0:T(1024)S(1)} %bitcast.104, f32[1250]{0:T(1024)S(1)} %get-tuple-element.134, ...), kind=kLoop, calls=%fused_computation.5.clone.1 | loop fusion | flops 100000000 | bytes 25798392 | tf_op jit(solution)/shard_map/while/body/jit(dynamic_update_index_in_dim)/dynamic_update_slice | solution.py:115
  285.7 22.0 %multiply_dynamic-update-slice_fusion.2 = f32[8,1250,5000]{2,1,0:T(8,128)} fusion(f32[8,1250,5000]{2,1,0:T(8,128)} %get-tuple-element.146, s32[]{:T(128)} %get-tuple-element.145, f32[5000]{0:T(1024)S(1)} %bitcast.103, f32[1250]{0:T(1024)S(1)} %get-tuple-element.132, f32[5000]{0:T(1024)S(1)} %bitcast.104, f32[1250]{0:T(1024)S(1)} %get-tuple-element.134, ...), kind=kLoop, calls=%fused_computation.5.clone.1 | loop fusion | flops 100000000 | bytes 25798392 | tf_op jit(solution)/shard_map/while/body/jit(dynamic_update_index_in_dim)/dynamic_update_slice | solution.py:115
  307.9 22.1 %multiply_dynamic-update-slice_fusion.2 = f32[8,1250,5000]{2,1,0:T(8,128)} fusion(f32[8,1250,5000]{2,1,0:T(8,128)} %get-tuple-element.146, s32[]{:T(128)} %get-tuple-element.145, f32[5000]{0:T(1024)S(1)} %bitcast.103, f32[1250]{0:T(1024)S(1)} %get-tuple-element.132, f32[5000]{0:T(1024)S(1)} %bitcast.104, f32[1250]{0:T(1024)S(1)} %get-tuple-element.134, ...), kind=kLoop, calls=%fused_computation.5.clone.1 | loop fusion | flops 100000000 | bytes 25798392 | tf_op jit(solution)/shard_map/while/body/jit(dynamic_update_index_in_dim)/dynamic_update_slice | solution.py:115
  330.1 22.1 %multiply_dynamic-update-slice_fusion.2 = f32[8,1250,5000]{2,1,0:T(8,128)} fusion(f32[8,1250,5000]{2,1,0:T(8,128)} %get-tuple-element.146, s32[]{:T(128)} %get-tuple-element.145, f32[5000]{0:T(1024)S(1)} %bitcast.103, f32[1250]{0:T(1024)S(1)} %get-tuple-element.132, f32[5000]{0:T(1024)S(1)} %bitcast.104, f32[1250]{0:T(1024)S(1)} %get-tuple-element.134, ...), kind=kLoop, calls=%fused_computation.5.clone.1 | loop fusion | flops 100000000 | bytes 25798392 | tf_op jit(solution)/shard_map/while/body/jit(dynamic_update_index_in_dim)/dynamic_update_slice | solution.py:115
  352.3 22.0 %multiply_dynamic-update-slice_fusion.2 = f32[8,1250,5000]{2,1,0:T(8,128)} fusion(f32[8,1250,5000]{2,1,0:T(8,128)} %get-tuple-element.146, s32[]{:T(128)} %get-tuple-element.145, f32[5000]{0:T(1024)S(1)} %bitcast.103, f32[1250]{0:T(1024)S(1)} %get-tuple-element.132, f32[5000]{0:T(1024)S(1)} %bitcast.104, f32[1250]{0:T(1024)S(1)} %get-tuple-element.134, ...), kind=kLoop, calls=%fused_computation.5.clone.1 | loop fusion | flops 100000000 | bytes 25798392 | tf_op jit(solution)/shard_map/while/body/jit(dynamic_update_index_in_dim)/dynamic_update_slice | solution.py:115
  374.4 22.1 %multiply_dynamic-update-slice_fusion.2 = f32[8,1250,5000]{2,1,0:T(8,128)} fusion(f32[8,1250,5000]{2,1,0:T(8,128)} %get-tuple-element.146, s32[]{:T(128)} %get-tuple-element.145, f32[5000]{0:T(1024)S(1)} %bitcast.103, f32[1250]{0:T(1024)S(1)} %get-tuple-element.132, f32[5000]{0:T(1024)S(1)} %bitcast.104, f32[1250]{0:T(1024)S(1)} %get-tuple-element.134, ...), kind=kLoop, calls=%fused_computation.5.clone.1 | loop fusion | flops 100000000 | bytes 25798392 | tf_op jit(solution)/shard_map/while/body/jit(dynamic_update_index_in_dim)/dynamic_update_slice | solution.py:115
  396.6 42.1 %all-gather = s32[32,1,128]{2,1,0:T(1,128)S(1)} all-gather(s32[1,1,128]{2,1,0:T(1,128)S(1)} %bitcast.113), channel_id=1, replica_groups=mesh['grp'=4,'dev'=8] {'grp','dev'}, dimensions={0}, use_global_device_ids=true | all-gather | bytes 16896 | tf_op jit(solution)/shard_map/all_gather | solution.py:101
  438.7 161.8 %reshape.330 = f32[10000,5000]{1,0:T(8,128)} reshape(f32[8,1250,5000]{2,1,0:T(8,128)} %get-tuple-element.55) | data formatting | bytes 400000000 | tf_op jit(solution)/shard_map/reshape | solution.py:115
  601.1 1.4 reduce.6
  602.8 4.5 scatter_custom_fusion.1
  607.3 6.0 slice_add_fusion
  613.3 2.8 gather_fusion.1
  616.1 42.8 %all_gather.13 = f32[4096,3]{1,0:T(8,128)S(1)} all-gather(f32[128,3]{1,0:T(8,128)S(1)} %gather_fusion.1), channel_id=1, replica_groups=mesh['grp'=4,'dev'=8] {'grp','dev'}, dimensions={0}, use_global_device_ids=true | all-gather | bytes 50688 | tf_op jit(solution)/shard_map/all_gather | solution.py:100
  658.9 25.4 %scatter_custom_fusion.2 = f32[10001,3]{1,0:T(8,128)} fusion(s32[4096]{0:T(1024)S(1)} %and_select_fusion, f32[4096,3]{1,0:T(8,128)S(1)} %all_gather.13, f32[]{:T(128)} %constant.63.clone.1), kind=kCustom, calls=%fused_computation.15 | custom fusion | flops 12288 | bytes 120016 | tf_op jit(solution)/shard_map/scatter-add | solution.py:105
  684.3 4.2 slice.57
  688.5 3.5 copy.97
  692.0 17.0 %all-gather.1 = f32[4,10000,3]{1,2,0:T(4,128)S(1)} all-gather(f32[1,10000,3]{1,2,0:T(4,128)S(1)} %bitcast.100), channel_id=1, replica_groups=mesh['grp'=4,'dev'=8] {'grp'}, dimensions={0}, use_global_device_ids=true | all-gather | bytes 600000 | tf_op jit(solution)/shard_map/all_gather | solution.py:121
  709.7 174.6 %fusion.19 = f32[3,10000]{1,0:T(4,128)} fusion(f32[10000,5000]{1,0:T(8,128)} %reshape.330, f32[40000,3]{0,1:T(4,128)S(1)} %reshape.321, s32[]{:T(128)S(6)} %select_n.21), kind=kOutput, calls=%fused_computation.41 | convolution fusion | flops 1800000000 | bytes 200201920 | tf_op jit(solution)/shard_map/dot_general | solution.py:123
  884.4 50.4 %all-reduce.5.cloned.1.call-done = f32[3,10000]{1,0:T(4,128)} async-done(((f32[3,10000]{1,0:T(4,128)}), f32[3,10000]{1,0:T(4,128)}) %all-reduce.5.cloned.1.call-update) | async-done | bytes 120016 | tf_op jit(solution)/shard_map/psum | solution.py:126
  934.7 1.1 fusion.15
  935.9 11.7 all-reduce.1
  947.6 1.2 multiply_reduce_fusion.1
  948.8 8.4 psum.45
  957.1 1.0 fusion.13
  958.2 15.7 %all-gather.2 = f32[4,10000,3]{1,2,0:T(4,128)S(1)} all-gather(f32[1,10000,3]{1,2,0:T(4,128)S(1)} %bitcast.101), channel_id=1, replica_groups=mesh['grp'=4,'dev'=8] {'grp'}, dimensions={0}, use_global_device_ids=true | all-gather | bytes 600000 | tf_op jit(solution)/shard_map/all_gather | solution.py:121
  974.0 0.6 reshape.323
  974.5 174.7 %fusion.17 = f32[3,10000]{1,0:T(4,128)} fusion(f32[10000,5000]{1,0:T(8,128)} %reshape.330, f32[40000,3]{0,1:T(4,128)S(1)} %reshape.323, s32[]{:T(128)S(6)} %select_n.21), kind=kOutput, calls=%fused_computation.39 | convolution fusion | flops 1800000000 | bytes 200201920 | tf_op jit(solution)/shard_map/dot_general | solution.py:123
  1149.2 52.6 %all-reduce.7.cloned.1.call-done = f32[3,10000]{1,0:T(4,128)} async-done(((f32[3,10000]{1,0:T(4,128)}), f32[3,10000]{1,0:T(4,128)}) %all-reduce.7.cloned.1.call-update) | async-done | bytes 120016 | tf_op jit(solution)/shard_map/psum | solution.py:126
  1201.9 1.1 multiply_reduce_fusion
  1203.0 3.5 copy.84
  1206.5 11.7 psum.47
  1218.1 0.8 fusion.16
  (62 shorter events, 4.5 us)
Async XLA Ops:
  7.2 211.3 %copy-start = (f32[3,40000]{1,0:T(4,128)S(1)}, f32[3,40000]{1,0:T(4,128)}, u32[]{:S(2)}) copy-start(f32[3,40000]{1,0:T(4,128)} %param.25) | copy-start | bytes 1440004
  7.2 25.9 %copy-start.1 = (s32[512,64]{0,1:T(8,128)S(1)}, s32[512,64]{0,1:T(8,128)}, u32[]{:S(2)}) copy-start(s32[512,64]{0,1:T(8,128)} %param.20) | copy-start | bytes 393220
  7.2 203.6 %copy-start.3 = (s32[8,64]{1,0:T(8,128)S(1)}, s32[8,64]{1,0:T(8,128)}, u32[]{:S(2)}) copy-start(s32[8,64]{1,0:T(8,128)} %param.21) | copy-start | bytes 6148
  212.8 387.8 %all-to-all-start = ((f32[8,1,192]{2,1,0:T(1,128)}), f32[8,1,192]{2,1,0:T(1,128)}, u32[]{:S(2)}, u32[]{:S(2)}) async-start(f32[8,1,192]{2,1,0:T(1,128)} %reshape.340), calls=%async_computation | async-start | bytes 16384 | tf_op jit(solution)/shard_map/all_to_all | solution.py:92
  217.9 716.8 %all-reduce.5.cloned.1.call-start = ((), (), s32[]{:S(2)}) async-start(), calls=%async_computation.1 | async-start | bytes 323584 | tf_op jit(solution)/shard_map/psum | solution.py:126
  218.9 177.6 %copy-start.4 = (s32[128]{0:T(128)S(1)}, s32[128]{0:T(128)}, u32[]{:S(2)}) copy-start(s32[128]{0:T(128)} %param.24) | copy-start | bytes 1540
  218.9 219.8 %copy-start.5 = (s32[128]{0:T(128)S(1)}, s32[128]{0:T(128)}, u32[]{:S(2)}) copy-start(s32[128]{0:T(128)} %param.23) | copy-start | bytes 1540
  438.7 161.8 %copy-start.2 = (s32[8,64]{1,0:T(8,128)S(1)}, s32[8,64]{1,0:T(8,128)}, u32[]{:S(2)}) copy-start(s32[8,64]{1,0:T(8,128)} %param.22) | copy-start | bytes 6148
  884.3 317.5 %all-reduce.7.cloned.1.call-start = ((), (), s32[]{:S(2)}) async-start(), calls=%async_computation.2 | async-start | bytes 323584 | tf_op jit(solution)/shard_map/psum | solution.py:126
Sparse Core Ops, SparseCore 0:
  884.5 50.2 all-reduce.4
  1149.3 52.4 all-reduce.6
where the time goes:
time: 1230 us
  other arithmetic  397 us (32%)
  matrix products  357 us (29%)
  local copies, waits for them, and re-layouts  199 us (16%)
  blocking collectives  149 us (12%)
  waiting for transfers between devices  103 us (8%)
  between operations  14.8 us (1%)
    dot_general x2, matrix products, on_device(): lax.dot_general(fetched, kernel_tile, contract, precision=lax.Precision.H...  349 us
    dynamic_update_slice x8, other arithmetic, on_device(): kernel_tile = lax.map(kernel_part, row_parts).reshape(block_rows, tile_cols)  177 us
    scatter-add x1, other arithmetic, element_partials(): jax.ops.segment_sum(partials.transpose(0, 2, 1).reshape(elements * elem_n...  177 us
    reshape x1, local copies, waits for them, and re-layouts, on_device(): kernel_tile = lax.map(kernel_part, row_parts).reshape(block_rows, tile_cols)  162 us
    psum x2, waiting for transfers between devices, on_device(): image = lax.psum(partial_value, 'dev') + ridge_weight * direction  103 us
    all_gather x1, blocking collectives, on_device(): values = lax.all_gather(surface_values, ('grp', 'dev'), axis=0, tiled=True)  42.8 us
    all_gather x1, blocking collectives, on_device(): points = lax.all_gather(surface_point, ('grp', 'dev'), axis=0, tiled=True)  42.1 us
    all_gather x2, blocking collectives, on_device(): whole = lax.all_gather(direction, 'grp', axis=1, tiled=True)  32.7 us
  transfers between devices with their start and end apart: 3, of which 2 were waited for; matrix products, arithmetic and copies ran while one was open for 28% of the time, Pallas kernels for 0%

commit v1 on v0

v1 whole, which is shorter than its diff:
```python
import functools

import jax
import jax.numpy as jnp
from jax import lax
from jax.experimental import pallas as pl
from jax.experimental.pallas import tpu as pltpu
from jax.sharding import PartitionSpec as P

NCP = 40000
NOWN = 8192
WIDE = 256
OWN_HIGH = NOWN // WIDE
FEATURES = 64
RIDGE = 4.0
RADIUS = (168.0 / (4.18879 * NCP)) ** (1.0 / 3.0)
F32, BF16, I32 = jnp.float32, jnp.bfloat16, jnp.int32
EXACT = lax.Precision.HIGHEST
NT = (((1,), (1,)), ((), ()))
NN = (((1,), (0,)), ((), ()))


def up_to(value, step):
    return -(-value // step) * step


def rows_iota(shape):
    return lax.broadcasted_iota(I32, shape, 0)


def rounded(value):
    return value.astype(BF16).astype(F32)


def one_hot(index, count):
    return jnp.where(rows_iota((count, index.shape[1])) == index, 1.0, 0.0)


def spread(rows, index_high, count):
    hit = rows_iota((count, index_high.shape[1])) == index_high
    return [jnp.where(hit, row, 0.0) for row in rows]


def stacked_rows(rows):
    sub = rows_iota((8, rows[0].shape[1]))
    tile = jnp.zeros((8, rows[0].shape[1]), F32)
    for number, row in enumerate(rows):
        tile = jnp.where(sub == number, row, tile)
    return tile


def split_features(tile, left):
    sub = rows_iota(tile.shape)
    x = jnp.where(sub < 3, tile, 0.0)
    x1 = rounded(x)
    rest = x - x1
    x2 = rounded(rest)
    x3 = rest - x2
    norm = jnp.sum(x * x, axis=0, keepdims=True)
    n1 = rounded(norm)
    n2 = rounded(norm - n1)
    n3 = norm - n1 - n2
    if left:
        ends = jnp.where(sub == 3, n1, jnp.where(sub == 4, n2, jnp.where(sub == 5, n3, jnp.where(sub < 3, 1.0, 0.0))))
        parts = [-2.0 * part for part in (x1, x2, x1, x2, x3, x1)]
    else:
        ends = jnp.where(sub == 0, n1, jnp.where(sub == 1, n2, jnp.where(sub == 2, n3, jnp.where(sub < 6, 1.0, 0.0))))
        parts = [x1, x1, x2, x2, x1, x3]
    return jnp.concatenate(parts + [ends, jnp.zeros_like(ends)], axis=0)


def wendland_product(weights, left, right):
    squared = lax.dot_general(left, right, NN, preferred_element_type=F32)
    squared = jnp.maximum(squared, 1e-12)
    remaining = jnp.maximum(1.0 - squared * lax.rsqrt(squared), 0.0)
    second = remaining * remaining
    phi = second * second * (1.25 - remaining)
    high = phi.astype(BF16)
    low = (phi - high.astype(F32)).astype(BF16)
    return lax.dot_general(weights, high, NN, preferred_element_type=F32) + lax.dot_general(
        weights, low, NN, preferred_element_type=F32
    )


def split_weights(tile):
    sub = rows_iota(tile.shape)
    head = rounded(tile)
    return jnp.where(sub < 3, head, jnp.where(sub < 6, tile - head, 0.0)).astype(BF16)


def element_kernel(
    adjoint_ref, state_ref, interp_ref, flux_ref, metric_ref, geometry_ref, connect_ref, source_ref,
    nodal_ref, outgoing_ref, adjoint_quad, state_quad, metric_turned, weighted, values, nodes, sums,
    *, halo_high,
):
    basis, quad = interp_ref.shape
    elements, wide = adjoint_ref.shape
    variables = wide // basis
    directions, _, elem_nodes = geometry_ref.shape
    interp = interp_ref[...].astype(F32)
    none = jnp.zeros_like(interp)
    pair = jnp.concatenate([jnp.concatenate([interp, none], axis=1), jnp.concatenate([none, interp], axis=1)], axis=0)
    pair = pair.T.astype(BF16)
    for source, target in ((adjoint_ref, adjoint_quad), (state_ref, state_quad)):
        for couple in range(variables // 2):
            target[couple * 2 * quad : (couple + 1) * 2 * quad, :] = lax.dot_general(
                pair, source[:, couple * 2 * basis : (couple + 1) * 2 * basis], NT, preferred_element_type=F32
            )
    metric_turned[...] = metric_ref[...].T
    nodes[...] = connect_ref[...].T

    def couple_rows(step, carry):
        start = pl.multiple_of(step * 8, 8)
        held = [state_quad[pl.ds(pl.multiple_of(w * quad + start, 8), 8), :] for w in range(variables)]
        metric = metric_turned[pl.ds(start, 8), :]
        for c in range(directions):
            total = None
            for v in range(variables):
                inner = flux_ref[c, v, 0] * held[0]
                for w in range(1, variables):
                    inner = inner + flux_ref[c, v, w] * held[w]
                term = adjoint_quad[pl.ds(pl.multiple_of(v * quad + start, 8), 8), :] * inner
                total = term if total is None else total + term
            weighted[c, pl.ds(start, 8), :] = total * metric
        return carry

    lax.fori_loop(0, quad // 8, couple_rows, 0)
    for c in range(directions):
        partial = lax.dot_general(geometry_ref[c].T, weighted[c], NN, precision=EXACT, preferred_element_type=F32)
        head = rounded(partial)
        values[2 * c] = head
        values[2 * c + 1] = partial - head
    sums[...] = jnp.zeros_like(sums)
    halo_rows = up_to(8 * halo_high, 16)

    def scatter_node(step, carry):
        total = None
        for part in range(2):
            row = step * 2 + part
            node = nodes[pl.ds(row, 1), :]
            low, high = node & (WIDE - 1), lax.shift_right_logical(node, 8)
            terms = [values[k, pl.ds(row, 1), :] for k in range(2 * directions)]
            pieces = spread(terms, high, OWN_HIGH)
            tile = stacked_rows(terms)
            for h in range(halo_rows // 8):
                pieces.append(jnp.where(high == OWN_HIGH + h, tile, 0.0))
            placed = jnp.concatenate(pieces, axis=0).astype(BF16)
            product = lax.dot_general(placed, one_hot(low, WIDE).astype(BF16), NT, preferred_element_type=F32)
            total = product if total is None else total + product
        sums[...] += total
        return carry

    lax.fori_loop(0, elem_nodes // 2, scatter_node, 0)
    for c in range(directions):
        first = 2 * c * OWN_HIGH
        nodal_ref[c] = sums[first : first + OWN_HIGH, :] + sums[first + OWN_HIGH : first + 2 * OWN_HIGH, :]
    base = 2 * directions * OWN_HIGH
    slots = source_ref.shape[1]
    outgoing_ref[...] = jnp.zeros_like(outgoing_ref)
    for peer in range(source_ref.shape[0]):
        source = source_ref[peer : peer + 1, :]
        low, high = source & (WIDE - 1), lax.shift_right_logical(source, 8)
        picked = None
        for h in range(halo_high):
            hot = jnp.where(high == h, one_hot(low, WIDE), 0.0)
            product = lax.dot_general(
                sums[base + 8 * h : base + 8 * h + 8, :], hot, NN, precision=EXACT, preferred_element_type=F32
            )
            picked = product if picked is None else picked + product
        for c in range(directions):
            outgoing_ref[peer, c : c + 1, 0:slots] = picked[2 * c : 2 * c + 1] + picked[2 * c + 1 : 2 * c + 2]


def points_kernel(coords_ref, slot_ref, tiles_ref, surface_ref, table, *, groups, members, share):
    count = groups * members
    block = tiles_ref.shape[1] // count
    group_rows = coords_ref.shape[1] // groups
    tiles_ref[...] = jnp.full_like(tiles_ref, 1e3)
    for k in range(count):
        start = (k // members) * group_rows + (k % members) * share
        length = min(share, group_rows - (k % members) * share)
        if length > 0:
            tiles_ref[0:3, k * block : k * block + length] = (coords_ref[:, start : start + length] - 0.5) * (1.0 / RADIUS)
    highs = count * block // WIDE
    for h in range(highs):
        for c in range(3):
            table[c, h : h + 1, :] = tiles_ref[c : c + 1, h * WIDE : (h + 1) * WIDE]
    slot = slot_ref[...]
    low, high = slot & (WIDE - 1), lax.shift_right_logical(slot, 8)
    hot = one_hot(low, WIDE)
    place = one_hot(high, highs)
    rows = []
    for c in range(3):
        chosen = lax.dot_general(table[c], hot, NN, precision=EXACT, preferred_element_type=F32)
        rows.append(jnp.sum(chosen * place, axis=0, keepdims=True))
    surface_ref[...] = stacked_rows(rows)


def own_kernel(incoming_ref, target_ref, nodal_ref, node_ref, slot_ref, surface_ref, owned_ref, payload_ref):
    directions = nodal_ref.shape[0]
    slots = target_ref.shape[1]
    total = None
    for peer in range(target_ref.shape[0]):
        target = target_ref[peer : peer + 1, :]
        low, high = target & (WIDE - 1), lax.shift_right_logical(target, 8)
        terms = []
        for c in range(directions):
            value = incoming_ref[peer, c : c + 1, 0:slots]
            head = rounded(value)
            terms += [head, value - head]
        placed = jnp.concatenate(spread(terms, high, OWN_HIGH), axis=0).astype(BF16)
        product = lax.dot_general(placed, one_hot(low, WIDE).astype(BF16), NT, preferred_element_type=F32)
        total = product if total is None else total + product
    node = node_ref[...]
    low, high = node & (WIDE - 1), lax.shift_right_logical(node, 8)
    hot = one_hot(low, WIDE)
    place = one_hot(high, OWN_HIGH)
    rows = []
    for c in range(directions):
        first = 2 * c * OWN_HIGH
        owned = nodal_ref[c] + (total[first : first + OWN_HIGH] + total[first + OWN_HIGH : first + 2 * OWN_HIGH])
        for h in range(OWN_HIGH):
            owned_ref[c : c + 1, h * WIDE : (h + 1) * WIDE] = owned[h : h + 1, :]
        chosen = lax.dot_general(owned, hot, NN, precision=EXACT, preferred_element_type=F32)
        rows.append(jnp.sum(chosen * place, axis=0, keepdims=True))
    index = slot_ref[...].astype(F32)
    surface = surface_ref[...]
    tile = stacked_rows([surface[0:1], surface[1:2], surface[2:3]] + rows + [index])
    payload_ref[...] = jnp.broadcast_to(tile[None], payload_ref.shape)


def first_image_kernel(rank_ref, payload_ref, tiles_ref, right_ref, image_ref, sums, own_right, image, left_scratch, weights):
    count, _, surface = payload_ref.shape
    block = right_ref.shape[2]
    highs = count * block // WIDE
    together = 4
    rank = rank_ref[0]
    sums[...] = jnp.zeros_like(sums)

    def gather_rows(step, carry):
        tiles = [payload_ref[step * together + part] for part in range(together)]
        tile = jnp.concatenate(tiles, axis=1)
        slot = tile[6:7].astype(I32)
        low, high = slot & (WIDE - 1), lax.shift_right_logical(slot, 8)
        terms = []
        for c in range(3):
            head = rounded(tile[3 + c : 4 + c])
            terms += [head, tile[3 + c : 4 + c] - head]
        placed = jnp.concatenate(spread(terms, high, highs), axis=0).astype(BF16)
        sums[...] += lax.dot_general(placed, one_hot(low, WIDE).astype(BF16), NT, preferred_element_type=F32)
        left_scratch[pl.ds(pl.multiple_of(step * together * surface, 128), together * surface), :] = split_features(
            tile, True
        ).T.astype(BF16)
        doubled = stacked_rows([tile[3 + c : 4 + c] for c in range(3)] * 2)
        weights[:, pl.ds(pl.multiple_of(step * together * surface, 128), together * surface)] = split_weights(doubled)
        return carry

    lax.fori_loop(0, count // together, gather_rows, 0)
    per = block // WIDE
    for h in range(highs):
        for c in range(3):
            first = 2 * c * highs + h
            right_ref[h // per, c : c + 1, (h % per) * WIDE : (h % per + 1) * WIDE] = (
                sums[first : first + 1, :] + sums[first + highs : first + highs + 1, :]
            )
    own_right[...] = right_ref[rank]
    for j in range(per):
        start = pl.multiple_of(rank * block + j * WIDE, WIDE)
        right = split_features(tiles_ref[:, pl.ds(start, WIDE)], False).astype(BF16)

        def accumulate(step, total):
            begin = pl.multiple_of(step * WIDE, WIDE)
            return total + wendland_product(weights[:, pl.ds(begin, WIDE)], left_scratch[pl.ds(begin, WIDE), :], right)

        total = lax.fori_loop(0, count * surface // WIDE, accumulate, jnp.zeros((8, WIDE), F32))
        lanes = slice(j * WIDE, (j + 1) * WIDE)
        for c in range(3):
            image[c : c + 1, lanes] = 4.0 * (total[c : c + 1] + total[3 + c : 4 + c]) + RIDGE * own_right[c : c + 1, lanes]
    image_ref[...] = jnp.broadcast_to(image[...][None], image_ref.shape)


def curvature_kernel(rank_ref, right_ref, image_ref, tiles_ref, direction_ref, scalars_ref, curve_ref, doubled, left_scratch, weights):
    count, _, block = right_ref.shape
    rank = rank_ref[0]

    def total_of(values):
        return jnp.sum(jnp.sum(values, axis=0), axis=1, keepdims=True)

    right, image = right_ref[...], image_ref[...]
    norm = total_of(right * right)
    step_size = norm / total_of(right * image)
    residual = right - step_size[None] * image
    norm_next = total_of(residual * residual)
    direction = residual + (norm_next / norm)[None] * right
    direction_ref[...] = direction
    doubled[...] = jnp.zeros_like(doubled)
    doubled[:, 0:3, :] = direction
    doubled[:, 3:6, :] = direction
    scalars_ref[...] = jnp.zeros_like(scalars_ref)
    scalars_ref[0:3, :] = jnp.broadcast_to(step_size, (3, 128))
    scalars_ref[3:6, :] = jnp.broadcast_to(norm_next, (3, 128))
    per = block // WIDE
    own = doubled[rank]
    weights[...] = split_weights(own)
    for i in range(per):
        start = pl.multiple_of(rank * block + i * WIDE, WIDE)
        left_scratch[i * WIDE : (i + 1) * WIDE, :] = split_features(tiles_ref[:, pl.ds(start, WIDE)], True).T.astype(BF16)
    half = count // 2

    def columns(step, total):
        offset = step // per
        lane = pl.multiple_of((step - offset * per) * WIDE, WIDE)
        owner = lax.rem(rank + offset, count)
        right = split_features(tiles_ref[:, pl.ds(pl.multiple_of(owner * block + lane, WIDE), WIDE)], False).astype(BF16)
        product = None
        for i in range(per):
            term = wendland_product(weights[:, i * WIDE : (i + 1) * WIDE], left_scratch[i * WIDE : (i + 1) * WIDE, :], right)
            product = term if product is None else product + term
        factor = jnp.where((offset == 0) | (offset == half), 1.0, 2.0)
        return total + factor * (product * doubled[owner, :, pl.ds(lane, WIDE)])

    total = lax.fori_loop(0, (half + 1) * per, columns, jnp.zeros((8, WIDE), F32))
    sub = rows_iota(own.shape)
    ridge = RIDGE * jnp.sum(jnp.where(sub < 3, own * own, 0.0), axis=1, keepdims=True)
    curve = 4.0 * jnp.sum(total, axis=1, keepdims=True) + ridge
    curve_ref[...] = jnp.broadcast_to(curve[None], curve_ref.shape)


def finish_kernel(rank_ref, curve_ref, scalars_ref, right_ref, direction_ref, point_ref, *, members, share):
    curve = jnp.sum(curve_ref[...], axis=0)
    curve = curve[0:3] + curve[3:6]
    step_size = scalars_ref[0:3, 0:1]
    second = scalars_ref[3:6, 0:1] / curve[:, 0:1]
    first_block = (rank_ref[0] // members) * members
    total = point_ref.shape[1]
    for member in range(members):
        length = min(share, total - member * share)
        if length > 0:
            value = step_size * right_ref[first_block + member] + second * direction_ref[first_block + member]
            point_ref[:, member * share : member * share + length] = value[:, 0:length]


def call(body, outs, scratch, scalars=(), **cost):
    def run(*operands):
        specs = [
            pl.BlockSpec(memory_space=pltpu.SMEM if number in scalars else pltpu.VMEM) for number in range(len(operands))
        ]
        return pl.pallas_call(
            body,
            out_shape=[jax.ShapeDtypeStruct(shape, F32) for shape in outs],
            in_specs=specs,
            out_specs=[pl.BlockSpec(memory_space=pltpu.VMEM)] * len(outs),
            scratch_shapes=[pltpu.VMEM(shape, kind) for shape, kind in scratch],
            compiler_params=pltpu.CompilerParams(vmem_limit_bytes=48 << 20),
            cost_estimate=pl.CostEstimate(transcendentals=0, **cost),
        )(*operands)

    return run


def on_device(
    adjoint, state, interp, flux_weights, metric, geometry, connectivity, halo_source, halo_target,
    surface_node, surface_point, point_coords,
):
    members, groups = lax.axis_size("dev"), lax.axis_size("grp")
    count = members * groups
    both = ("grp", "dev")
    rank = (lax.axis_index("grp") * members + lax.axis_index("dev")).astype(I32).reshape(1)
    halo_count = halo_source.shape[1] * (members - 1) // 2
    halo_high = halo_count // WIDE + 1
    elements = adjoint.shape[0]
    basis, quad = interp.shape
    wide = adjoint.shape[1] // basis * quad
    elem_nodes = geometry.shape[2]
    surface = surface_node.shape[0]
    group_rows = NCP // groups
    share = -(-group_rows // members)
    block = up_to(share, WIDE)
    highs = count * block // WIDE
    in_group = surface_point % group_rows
    slot = (surface_point // group_rows * members + in_group // share) * block + in_group % share
    slot = slot.reshape(1, surface)
    node = surface_node.reshape(1, surface)
    halo_rows = up_to(8 * halo_high, 16)

    nodal, outgoing = call(
        functools.partial(element_kernel, halo_high=halo_high),
        [(3, OWN_HIGH, WIDE), (members, 8, 128)],
        [
            ((wide, elements), F32), ((wide, elements), F32), ((quad, elements), F32), ((3, quad, elements), F32),
            ((6, elem_nodes, elements), F32), ((elem_nodes, elements), I32), ((6 * OWN_HIGH + halo_rows, WIDE), F32),
        ],
        scalars=(3,), flops=10**10, bytes_accessed=2 * 10**6,
    )(adjoint, state, interp, flux_weights, metric, geometry, connectivity, halo_source)
    incoming = lax.all_to_all(outgoing, "dev", split_axis=0, concat_axis=0, tiled=True)
    tiles, surface_tile = call(
        functools.partial(points_kernel, groups=groups, members=members, share=share),
        [(8, count * block), (8, surface)],
        [((3, highs, WIDE), F32)],
        flops=10**9, bytes_accessed=2 * 10**6,
    )(point_coords, slot)
    owned, payload = call(
        own_kernel, [(3, NOWN), (count, 8, surface)], [], flops=10**9, bytes_accessed=10**6
    )(incoming, halo_target, nodal, node, slot, surface_tile)
    payload = lax.all_to_all(payload, both, split_axis=0, concat_axis=0, tiled=True)
    right_side, image = call(
        first_image_kernel,
        [(count, 3, block), (count, 3, block)],
        [
            ((6 * highs, WIDE), F32), ((3, block), F32), ((3, block), F32),
            ((count * surface, FEATURES), BF16), ((8, count * surface), BF16),
        ],
        scalars=(0,), flops=10**10, bytes_accessed=4 * 10**6,
    )(rank, payload, tiles)
    image = lax.all_to_all(image, both, split_axis=0, concat_axis=0, tiled=True)
    direction, scalars, curve = call(
        curvature_kernel,
        [(count, 3, block), (8, 128), (count, 8, 1)],
        [((count, 8, block), F32), ((block, FEATURES), BF16), ((8, block), BF16)],
        scalars=(0,), flops=5 * 10**10, bytes_accessed=4 * 10**6,
    )(rank, right_side, image, tiles)
    curve = lax.all_to_all(curve, both, split_axis=0, concat_axis=0, tiled=True)
    (solution_rows,) = call(
        functools.partial(finish_kernel, members=members, share=share),
        [(3, group_rows)], [], scalars=(0,), flops=10**6, bytes_accessed=2 * 10**6,
    )(rank, curve, scalars, right_side, direction)
    return (owned, solution_rows)


def solution(mesh):
    shard = P(("grp", "dev"), None)
    line = P(("grp", "dev"))
    return jax.shard_map(
        on_device,
        mesh=mesh,
        in_specs=(shard, shard, P(), P(), shard, P(), shard, shard, shard, line, line, P()),
        out_specs=(P(None, ("grp", "dev")), P(None, "grp")),
        check_vma=False,
    )
```

time: 1230 us -> 190 us (0.15)
  other arithmetic: 397 us -> 0.03 us
  matrix products: 357 us -> 0 us
  local copies, waits for them, and re-layouts: 199 us -> 7.57 us
  Pallas kernels: 0 us -> 130 us
  blocking collectives: 149 us -> 30.2 us
  waiting for transfers between devices: 103 us -> 11.8 us
  between operations: 14.8 us -> 0.72 us
    dot_general x6 -> x0, matrix products: 357 us -> none  [the longest x2 349 us: on_device(): lax.dot_general(fetched, kernel_tile, contract, precision=lax.Precision.H...]
    scatter-add x3 -> x0, other arithmetic: 207 us -> none  [the longest x1 177 us: element_partials(): jax.ops.segment_sum(partials.transpose(0, 2, 1).reshape(elements * elem_n...]
    dynamic_update_slice x8 -> x0, other arithmetic: 177 us -> none  [on_device(): kernel_tile = lax.map(kernel_part, row_parts).reshape(block_rows, tile_cols)]
    reshape x4 -> x0, local copies, waits for them, and re-layouts: 176 us -> none  [the longest x1 162 us: on_device(): kernel_tile = lax.map(kernel_part, row_parts).reshape(block_rows, tile_cols)]
    pallas_call x0 -> x6, Pallas kernels: none -> 130 us  [run(): pl.pallas_call(body, out_shape=[jax.ShapeDtypeStruct(shape, F32) for shap...]
    all_gather x4 -> x0, blocking collectives: 118 us -> none  [the longest x1 42.8 us: on_device(): values = lax.all_gather(surface_values, ('grp', 'dev'), axis=0, tiled=True)]
    psum x2 -> x0, waiting for transfers between devices: 103 us -> none  [on_device(): image = lax.psum(partial_value, 'dev') + ridge_weight * direction]
    psum x3 -> x0, blocking collectives: 31.7 us -> none  [the longest x2 20.1 us: squares(): return lax.psum(jnp.sum(residual * residual, axis=1), 'grp')]
  transfers between devices with their start and end apart: 3 -> 2, of which waited for: 2 -> 2; matrix products, arithmetic and copies ran while one was open for 28% -> 0% of each run, Pallas kernels for 0% -> 1%
where the time goes in v1:
time: 190 us; the launch traced here: 189 us
  Pallas kernels  130 us (68%)
  blocking collectives  30.2 us (16%)
  waiting for transfers between devices  11.8 us (6%)
  starting transfers between devices  9.14 us (5%)
  local copies, waits for them, and re-layouts  7.57 us (4%)
    pallas_call x6, Pallas kernels, run(): pl.pallas_call(body, out_shape=[jax.ShapeDtypeStruct(shape, F32) for shap...  130 us
    all_to_all x1, blocking collectives, on_device(): image = lax.all_to_all(image, both, split_axis=0, concat_axis=0, tiled=True)  19.7 us
    all_to_all x1, blocking collectives, on_device(): curve = lax.all_to_all(curve, both, split_axis=0, concat_axis=0, tiled=True)  10.5 us
    all_to_all x1, waiting for transfers between devices, on_device(): lax.all_to_all(payload, both, split_axis=0, concat_axis=0, tiled=True)  8.22 us
    unnamed x22, local copies, waits for them, and re-layouts  7.07 us
    all_to_all x1, starting transfers between devices, on_device(): lax.all_to_all(outgoing, 'dev', split_axis=0, concat_axis=0, tiled=True)  5.1 us
    all_to_all x1, starting transfers between devices, on_device(): lax.all_to_all(payload, both, split_axis=0, concat_axis=0, tiled=True)  4.03 us
  transfers between devices with their start and end apart: 2, of which 2 were waited for; matrix products, arithmetic and copies ran while one was open for 0% of the time, Pallas kernels for 1%

profile of v1, /device:TPU:0, one launch (start us, length us, event | category | flops | bytes accessed | tf_op | source)
XLA Modules:
  0.0 189.2 jit_solution(12432312090291588001)
XLA Ops:
  0.6 1.0 copy.16.metric_ref
  1.7 1.0 copy.17.connect_ref
  2.7 0.0 copy-start.1
  2.7 1.0 copy-done.1
  3.7 0.0 copy-start.2
  3.7 1.0 copy-done.2
  4.7 0.0 copy-start.3
  4.7 0.9 copy-done.3
  5.6 0.0 copy-start.4
  5.6 0.7 copy-done.4
  6.3 0.0 copy-start.5
  6.3 0.7 copy-done.5
  7.0 0.0 copy-start.6
  7.0 0.7 copy-done.6
  7.7 0.0 copy-start.9
  7.7 0.0 copy-start
  7.7 15.9 %shard_map.131 = (f32[3,32,256]{2,1,0:T(8,128)S(1)}, f32[8,8,128]{2,1,0:T(8,128)}) custom-call(bf16[512,384]{1,0:T(8,128)(2,1)S(1)} %copy-done.1, bf16[512,384]{1,0:T(8,128)(2,1)S(1)} %copy-done.2, bf16[64,64]{1,0:T(8,128)(2,1)S(1)} %copy-done.4, f32[3,6,6]{2,1,0:T(8,128)S(1)} %copy-done.5, f32[512,64]{1,0:T(8,128)S(1)} %copy.16.metric_ref, ...), custom_call_target="tpu_custom_call" | custom-call | flops 10000000000 | bytes 2000000 | tf_op jit(solution)/shard_map/pallas_call | solution.py:348
  23.6 5.1 %all-to-all-start = ((f32[8,8,128]{2,1,0:T(8,128)}), f32[8,8,128]{2,1,0:T(8,128)S(1)}, u32[]{:S(2)}, u32[]{:S(2)}) async-start(f32[8,8,128]{2,1,0:T(8,128)} %get-tuple-element.13), calls=%async_computation | async-start | bytes 65536 | tf_op jit(solution)/shard_map/all_to_all | solution.py:395
  28.7 0.0 copy-done.9
  28.7 0.0 copy-done
  28.7 0.0 copy-start.7
  28.7 0.0 copy-start.8
  28.8 1.1 shard_map.132
  29.9 3.6 %all-to-all-done.incoming_ref = f32[8,8,128]{2,1,0:T(8,128)S(1)} async-done(((f32[8,8,128]{2,1,0:T(8,128)}), f32[8,8,128]{2,1,0:T(8,128)S(1)}, u32[]{:S(2)}, u32[]{:S(2)}) %all-to-all-start) | async-done | bytes 32800 | tf_op jit(solution)/shard_map/all_to_all | solution.py:395
  33.5 0.0 copy-done.7
  33.5 0.0 copy-done.8
  33.5 1.6 shard_map.133
  35.1 4.0 %all-to-all-start.1 = ((f32[32,8,128]{2,1,0:T(8,128)}), f32[32,8,128]{2,1,0:T(8,128)S(1)}, u32[]{:S(2)}, u32[]{:S(2)}) async-start(f32[32,8,128]{2,1,0:T(8,128)} %get-tuple-element.17), calls=%async_computation.1 | async-start | bytes 262144 | tf_op jit(solution)/shard_map/all_to_all | solution.py:405
  39.2 8.2 %all-to-all-done.1.payload_ref = f32[32,8,128]{2,1,0:T(8,128)S(1)} async-done(((f32[32,8,128]{2,1,0:T(8,128)}), f32[32,8,128]{2,1,0:T(8,128)S(1)}, u32[]{:S(2)}, u32[]{:S(2)}) %all-to-all-start.1) | async-done | bytes 131104 | tf_op jit(solution)/shard_map/all_to_all | solution.py:405
  47.4 36.0 %shard_map.134 = (f32[32,3,1280]{2,1,0:T(4,128)S(1)}, f32[32,3,1280]{2,1,0:T(4,128)S(1)}) custom-call(s32[1]{0:T(128)} %bitcast.2.rank_ref, f32[32,8,128]{2,1,0:T(8,128)S(1)} %all-to-all-done.1.payload_ref, f32[8,40960]{1,0:T(8,128)S(1)} %get-tuple-element.18.tiles_ref), custom_call_target="tpu_custom_call" | custom-call | flops 10000000000 | bytes 4000000 | tf_op jit(solution)/shard_map/pallas_call | solution.py:348
  83.4 19.7 %all_to_all.20.image_ref = f32[32,3,1280]{2,1,0:T(4,128)S(1)} all-to-all(f32[32,3,1280]{2,1,0:T(4,128)S(1)} %get-tuple-element.20), channel_id=1, replica_groups=mesh['grp'=4,'dev'=8] {'grp','dev'}, dimensions={0} | all-to-all | bytes 983040 | tf_op jit(solution)/shard_map/all_to_all | solution.py:415
  103.1 74.2 %shard_map.135 = (f32[32,3,1280]{2,1,0:T(4,128)S(1)}, f32[8,128]{1,0:T(8,128)S(1)}, f32[32,8,1]{2,1,0:T(8,128)S(1)}) custom-call(s32[1]{0:T(128)} %bitcast.2.rank_ref, f32[32,3,1280]{2,1,0:T(4,128)S(1)} %get-tuple-element.19.right_ref, f32[32,3,1280]{2,1,0:T(4,128)S(1)} %all_to_all.20.image_ref, f32[8,40960]{1,0:T(8,128)S(1)} %get-tuple-element.18.tiles_ref), custom_call_target="tpu_custom_call" | custom-call | flops 49999998976 | bytes 4000000 | tf_op jit(solution)/shard_map/pallas_call | solution.py:348
  177.3 0.2 copy.18
  177.5 10.5 %all_to_all.21 = f32[32,8,1]{1,2,0:T(1,128)S(1)} all-to-all(f32[32,8,1]{1,2,0:T(1,128)S(1)} %copy.18), channel_id=1, replica_groups=mesh['grp'=4,'dev'=8] {'grp','dev'}, dimensions={0} | all-to-all | bytes 2048 | tf_op jit(solution)/shard_map/all_to_all | solution.py:422
  188.0 0.3 copy.19.curve_ref
  188.3 0.9 shard_map.136
  (1 shorter events, 0.0 us)
Async XLA Ops:
  2.7 1.0 copy-start.1
  3.7 1.0 copy-start.2
  4.7 0.9 copy-start.3
  5.6 0.7 copy-start.4
  6.3 0.7 copy-start.5
  7.0 0.7 copy-start.6
  7.7 21.0 %copy-start.9 = (s32[128]{0:T(128)S(1)}, s32[128]{0:T(128)}, u32[]{:S(2)}) copy-start(s32[128]{0:T(128)} %param.22) | copy-start | bytes 1540
  7.7 21.0 %copy-start = (f32[3,40000]{1,0:T(4,128)S(1)}, f32[3,40000]{1,0:T(4,128)}, u32[]{:S(2)}) copy-start(f32[3,40000]{1,0:T(4,128)} %coords_ref.1) | copy-start | bytes 1440004
  23.6 9.9 %all-to-all-start = ((f32[8,8,128]{2,1,0:T(8,128)}), f32[8,8,128]{2,1,0:T(8,128)S(1)}, u32[]{:S(2)}, u32[]{:S(2)}) async-start(f32[8,8,128]{2,1,0:T(8,128)} %get-tuple-element.13), calls=%async_computation | async-start | bytes 65536 | tf_op jit(solution)/shard_map/all_to_all | solution.py:395
  28.7 4.8 %copy-start.7 = (s32[8,64]{1,0:T(8,128)S(1)}, s32[8,64]{1,0:T(8,128)}, u32[]{:S(2)}) copy-start(s32[8,64]{1,0:T(8,128)} %target_ref.1) | copy-start | bytes 6148
  28.7 4.8 %copy-start.8 = (s32[128]{0:T(128)S(1)}, s32[128]{0:T(128)}, u32[]{:S(2)}) copy-start(s32[128]{0:T(128)} %param.21) | copy-start | bytes 1540
  35.1 12.3 %all-to-all-start.1 = ((f32[32,8,128]{2,1,0:T(8,128)}), f32[32,8,128]{2,1,0:T(8,128)S(1)}, u32[]{:S(2)}, u32[]{:S(2)}) async-start(f32[32,8,128]{2,1,0:T(8,128)} %get-tuple-element.17), calls=%async_computation.1 | async-start | bytes 262144 | tf_op jit(solution)/shard_map/all_to_all | solution.py:405
